TPU v7x, 512 devices: a whole 4x4x16 slice. The times are simulated.
512 devices in a mesh: dp: 16 (over z), cls: 32 (over y, x, core).
Axes of the slice: x: 4, y: 4, z: 16, core: 2. Of those that a mesh axis runs over, the one named last changes fastest.
Arguments:
- features: bfloat16 [24576, 512], P(('dp', 'cls'))
- centers: float32 [1048576, 512], P(('dp', 'cls'))
- labels: int32 [24576], replicated, may hold values from 0 to 1048575, as said below
- sampled: int32 [512, 2], replicated, may hold values from 0 to 127, as said below
Outputs:
- losses: float32 [24576], P(('dp', 'cls'))
- feature_grad: float32 [24576, 512], P(('dp', 'cls'))
- center_grad: float32 [16384, 512], P(('dp', 'cls'))
Inputs may be any that keep to these rules, and one draw needn't show every extreme that they name: Each row of sampled names 2 different blocks of 16 classes of that device's 2048 classes. `labels`: every label is a class inside a block that its owning device lists in sampled.
All inputs are finite; a program needn't handle non-finite values.
Results may differ from a plain program's by a relative error of at most 0.0046.
Values may be sent and summed in bfloat16 or wider, within the bound.
A program may use at most 64 MiB of HBM per device.

v0:
```python
import jax
import jax.numpy as jnp
from jax import lax
from jax.sharding import PartitionSpec as P

BLK = 16


logit_scale = 64.0
cosine_margin = 0.35
norm_eps = 1e-06


def unit_rows(values):
    return values * lax.rsqrt(jnp.sum(values * values, axis=-1, keepdims=True) + norm_eps)


def class_ids_of(owners, blocks, block_count):
    offsets = jnp.arange(BLK, dtype=jnp.int32)
    return (
        (owners[:, None] * block_count + blocks)[:, :, None] * BLK + offsets[None, None, :]
    ).reshape(-1)


def margin_terms(gathered_x, gathered_w, class_ids, row_labels):
    cosine = lax.dot_general(
        gathered_x, gathered_w, (((1,), (1,)), ((), ())), preferred_element_type=jnp.float32
    )
    onehot = row_labels[:, None] == class_ids[None, :]
    scores = (
        logit_scale * cosine - logit_scale - jnp.where(onehot, logit_scale * cosine_margin, 0.0)
    )
    expz = jnp.exp(scores)
    return (expz, onehot, jnp.sum(expz, axis=1), jnp.sum(jnp.where(onehot, scores, 0.0), axis=1))


def logit_grad(expz, onehot, inverse):
    return ((expz * inverse[:, None] - onehot.astype(jnp.float32)) * logit_scale).astype(
        jnp.bfloat16
    )


def local(features, centers, labels, sampled):
    row_count, feat_width = features.shape
    dp_size = lax.axis_size("dp")
    cls_size = lax.axis_size("cls")
    dp_index = lax.axis_index("dp")
    cls_index = lax.axis_index("cls")
    block_count = centers.shape[0] // BLK
    sample_blocks = sampled.shape[1]
    table_all = sampled.reshape(dp_size, cls_size, sample_blocks)
    own_blocks = lax.dynamic_slice(
        table_all, (dp_index, cls_index, 0), (1, 1, sample_blocks)
    ).reshape(-1)
    chosen = centers.reshape(block_count, BLK, feat_width)[own_blocks].reshape(-1, feat_width)
    center_full, center_back = jax.vjp(unit_rows, chosen)
    center_unit = center_full.astype(jnp.bfloat16)
    feature_full, feature_back = jax.vjp(unit_rows, features.astype(jnp.float32))
    feature_unit = feature_full.astype(jnp.bfloat16)
    gathered_w = lax.all_gather(center_unit, "cls", axis=0, tiled=True)
    gathered_x = lax.all_gather(feature_unit, "dp", axis=0, tiled=True)
    line_blocks = lax.dynamic_slice(
        table_all, (dp_index, 0, 0), (1, cls_size, sample_blocks)
    ).reshape(cls_size, sample_blocks)
    owners = dp_index * cls_size + jnp.arange(cls_size, dtype=jnp.int32)
    class_ids = class_ids_of(owners, line_blocks, block_count)
    label_grid = labels.reshape(dp_size, cls_size, row_count)
    row_labels = lax.dynamic_slice_in_dim(label_grid, cls_index, 1, 1).reshape(-1)
    expz, onehot, totals, targets = margin_terms(gathered_x, gathered_w, class_ids, row_labels)
    all_total, all_target = lax.psum((totals, targets), "dp")
    inverse = 1.0 / all_total
    share_total = lax.dynamic_slice_in_dim(all_total, dp_index * row_count, row_count)
    share_target = lax.dynamic_slice_in_dim(all_target, dp_index * row_count, row_count)
    losses = jnp.log(share_total) - share_target
    grad_logit = logit_grad(expz, onehot, inverse)
    feature_term = lax.psum_scatter(
        jnp.dot(grad_logit, gathered_w, preferred_element_type=jnp.float32),
        "dp",
        scatter_dimension=0,
        tiled=True,
    )
    center_term = lax.psum_scatter(
        lax.dot_general(
            grad_logit, gathered_x, (((0,), (0,)), ((), ())), preferred_element_type=jnp.float32
        ),
        "cls",
        scatter_dimension=0,
        tiled=True,
    )
    feature_grad = feature_back(feature_term)[0]
    center_grad = center_back(center_term)[0]
    return (losses, feature_grad, center_grad)


def solution(mesh):
    placed = (P(("dp", "cls"), None), P(("dp", "cls"), None), P(), P())
    return jax.shard_map(
        local,
        mesh=mesh,
        in_specs=placed,
        out_specs=(P(("dp", "cls")), P(("dp", "cls"), None), P(("dp", "cls"), None)),
        check_vma=False,
    )
```

profile of v0, /device:TPU:1, one launch (start us, length us, event | category | flops | bytes accessed | tf_op | source)
XLA Modules:
  0.0 295.8 jit_solution(12827805074776610963)
XLA Ops:
  7.2 0.0 all-gather.2.cloned.1.call-start
  7.2 0.8 reshape.128
  8.0 0.1 constant_dynamic-slice_fusion.1
  8.1 0.1 copy.13
  8.2 2.7 gather_fusion
  10.9 0.1 multiply_reduce_fusion
  11.0 0.1 add.109
  11.1 0.7 fusion.8
  11.8 0.0 all-gather.2.cloned.1.call-update
  11.8 0.0 reduce-scatter.3.cloned.1.call-start
  11.9 0.1 copy.12
  12.0 0.1 iota_add_fusion
  12.1 0.1 add.117
  12.2 1.0 reshape.131
  13.3 0.1 eq.15
  13.4 0.9 fusion.5
  14.3 0.9 fusion.6
  15.2 36.3 %all_gather.6 = bf16[768,512]{1,0:T(8,128)(2,1)} all-gather(bf16[48,512]{1,0:T(8,128)(2,1)S(1)} %fusion.6), channel_id=1, replica_groups=mesh['dp'=16,'cls'=32] {'dp'}, dimensions={0}, use_global_device_ids=true | all-gather | bytes 835584 | tf_op jit(solution)/shard_map/all_gather | solution.py:61
  51.5 24.3 %all-gather.2.cloned.1.call-done = bf16[1024,512]{1,0:T(8,128)(2,1)} async-done(((bf16[32,512]{1,0:T(8,128)(2,1)}), bf16[1024,512]{1,0:T(8,128)(2,1)}) %all-gather.2.cloned.1.call-update) | async-done | bytes 1048592 | tf_op jit(solution)/shard_map/all_gather | solution.py:60
  75.8 3.0 %exponential_reduce_fusion = (f32[768]{0:T(1024)S(1)}, f32[768]{0:T(1024)S(1)}, f32[768,1024]{1,0:T(8,128)S(1)}) fusion(s32[1024]{0:T(1024)S(1)} %add.117, s32[768]{0:T(1024)S(1)} %eq.15, bf16[768,512]{1,0:T(8,128)(2,1)} %all_gather.6, bf16[1024,512]{1,0:T(8,128)(2,1)} %all-gather.2.cloned.1.call-done), kind=kOutput, calls=%fused_computation.9 | convolution fusion | flops 811596288 | bytes 4994048 | tf_op jit(solution)/shard_map/dot_general | solution.py:26
  78.8 25.1 %all-reduce = (f32[768]{0:T(1024)S(1)}, f32[768]{0:T(1024)S(1)}) all-reduce(f32[768]{0:T(1024)S(1)} %get-tuple-element.4, f32[768]{0:T(1024)S(1)} %get-tuple-element.3), channel_id=1, replica_groups=mesh['dp'=16,'cls'=32] {'dp'}, use_global_device_ids=true, to_apply=%region_5.6 | all-reduce | flops 1536 | bytes 12288 | tf_op jit(solution)/shard_map/psum | solution.py:70
  104.0 0.0 copy-start.3
  104.0 0.8 fusion.4
  104.8 0.0 copy-start
  104.8 1.2 copy-done
  106.0 0.0 copy-done.3
  106.0 0.0 copy-start.1
  106.0 2.1 fusion.11
  108.1 0.0 reduce-scatter.3.cloned.1.call-update
  108.2 0.0 copy-start.2
  108.2 0.0 reduce-scatter.5.cloned.1.call-start
  108.2 0.0 copy-done.1
  108.2 3.8 %fusion.12 = f32[1024,512]{1,0:T(8,128)} fusion(bf16[768,1024]{1,0:T(8,128)(2,1)} %copy-done, bf16[768,512]{1,0:T(8,128)(2,1)S(1)} %copy-done.1), kind=kOutput, calls=%fused_computation.41 | convolution fusion | flops 805306368 | bytes 4456448 | tf_op jit(solution)/shard_map/dot_general | solution.py:83
  112.0 0.0 reduce-scatter.5.cloned.1.call-update
  112.0 0.6 dynamic-slice_subtract_fusion
  112.6 59.0 %reduce-scatter.3.cloned.1.call-done = f32[48,512]{1,0:T(8,128)} async-done(((f32[768,512]{1,0:T(8,128)}), f32[48,512]{1,0:T(8,128)}) %reduce-scatter.3.cloned.1.call-update) | async-done | bytes 98320 | tf_op jit(solution)/shard_map/reduce_scatter | solution.py:76
  171.6 0.0 copy-done.2
  171.6 1.0 fusion.7
  172.7 112.5 %reduce-scatter.5.cloned.1.call-done = f32[32,512]{1,0:T(8,128)} async-done(((f32[1024,512]{1,0:T(8,128)}), f32[32,512]{1,0:T(8,128)}) %reduce-scatter.5.cloned.1.call-update) | async-done | bytes 65552 | tf_op jit(solution)/shard_map/reduce_scatter | solution.py:82
  285.2 1.0 fusion.9
  286.1 1.6 add_add_fusion
  287.8 1.6 add_add_fusion.1
  (12 shorter events, 0.1 us)
Async XLA Ops:
  7.2 68.7 %all-gather.2.cloned.1.call-start = ((), (), s32[]{:S(2)}) async-start(), calls=%async_computation.2 | async-start | bytes 1081344 | tf_op jit(solution)/shard_map/all_gather | solution.py:60
  11.8 159.8 %reduce-scatter.3.cloned.1.call-start = ((), (), s32[]{:S(2)}) async-start(), calls=%async_computation.3 | async-start | bytes 1671168 | tf_op jit(solution)/shard_map/reduce_scatter | solution.py:76
  104.0 2.0 copy-start.3
  104.8 1.2 copy-start
  106.0 2.2 copy-start.1
  108.2 63.5 %copy-start.2 = (bf16[48,512]{1,0:T(8,128)(2,1)S(1)}, bf16[48,512]{1,0:T(8,128)(2,1)}, u32[]{:S(2)}) copy-start(bf16[48,512]{1,0:T(8,128)(2,1)} %param.4) | copy-start | bytes 147460
  108.2 177.0 %reduce-scatter.5.cloned.1.call-start = ((), (), s32[]{:S(2)}) async-start(), calls=%async_computation.4 | async-start | bytes 2162688 | tf_op jit(solution)/shard_map/reduce_scatter | solution.py:82
Sparse Core Ops, SparseCore 0:
  11.9 63.8 all-gather.1
  108.3 63.3 reduce-scatter.2
  176.7 108.4 reduce-scatter.4
where the time goes:
time: 297 us; the launch traced here: 296 us
  waiting for transfers between devices  196 us (66%)
  blocking collectives  61.4 us (21%)
  between operations  13.9 us (5%)
  other arithmetic  9.28 us (3%)
  matrix products  8.94 us (3%)
  local copies, waits for them, and re-layouts  6.29 us (2%)
    reduce_scatter x1, waiting for transfers between devices, local(): lax.psum_scatter(lax.dot_general(grad_logit, gathered_x, (((0,), (0,)), (...  113 us
    reduce_scatter x1, waiting for transfers between devices, local(): lax.psum_scatter(jnp.dot(grad_logit, gathered_w, preferred_element_type=j...  59 us
    all_gather x1, blocking collectives, local(): gathered_x = lax.all_gather(feature_unit, 'dp', axis=0, tiled=True)  36.3 us
    psum x1, blocking collectives, local(): all_total, all_target = lax.psum((totals, targets), 'dp')  25.1 us
    all_gather x1, waiting for transfers between devices, local(): gathered_w = lax.all_gather(center_unit, 'cls', axis=0, tiled=True)  24.3 us
  transfers between devices with their start and end apart: 3, of which 3 were waited for; matrix products, arithmetic and copies ran while one was open for 3% of the time, Pallas kernels for 0%

commit v1 on v0

v1 whole, which is shorter than its diff:
```python
import functools

import jax
import jax.numpy as jnp
from jax import lax
from jax.experimental import pallas as pl
from jax.experimental.pallas import tpu as pltpu
from jax.sharding import PartitionSpec as P

MESH = pl.DeviceIdType.MESH
BLK = 16
D = 512
ROWS = 48
CLS = 32
NZ = 16
NP = 16
SIDE = 4
BLOCKS = 128
TILE_ROWS = NP * ROWS
TILE_CLS = 2 * NZ * CLS

logit_scale = 64.0
cosine_margin = 0.35
norm_eps = 1e-06

DIRECT = (4, -4, 1, -1, 2, -2)
PASS_UP = (1, 2, 3, -1)
PASS_DOWN = (-1, -2, -3, 1)
FROM_LOW = (-1, 1, 2, 3)
FROM_HIGH = (1, -1, -2, -3)


def wrap(value, size):
    return lax.rem(value + size, size)


def kernel(
    feat_ref, centers_ref, label_ref, sampled_ref,
    loss_ref, fgrad_ref, cgrad_ref,
    cbuf, chosen, xa, wa, et, gt, tot, tgt,
    sib_out, sib_in, part, part_b, relay_in, relay8, relay_out, zfin,
    fval, fout, fin1, fout2, fin2,
    csem, z_send, z_recv, s_send, s_recv, a_send, a_recv, b_send, b_recv,
    t_send, t_recv, u_send, u_recv, cs_send, cs_recv,
    r_send, r_recv, q_send, q_recv, f_send, f_recv, h_send, h_recv,
):
    z = lax.axis_index("dp")
    cls = lax.axis_index("cls")
    core = lax.rem(cls, 2)
    yx = lax.div(cls, 2)
    y = lax.div(yx, SIDE)
    x = lax.rem(yx, SIDE)
    first = jnp.where(core == 0, y, x)
    second = jnp.where(core == 0, x, y)

    def chip(p1, p2):
        return jnp.where(core == 0, p1 * SIDE + p2, p2 * SIDE + p1)

    def zdev(d):
        return (wrap(z + d, NZ), cls)

    def pdev(slot):
        return (z, slot * 2 + core)

    sibling = (z, yx * 2 + 1 - core)
    started = []

    def send(src, dst, ssem, rsem, dev):
        copy = pltpu.make_async_remote_copy(
            src_ref=src, dst_ref=dst, send_sem=ssem, recv_sem=rsem,
            device_id=dev, device_id_type=MESH,
        )
        copy.start()
        started.append(copy)

    def arrived(dst, ssem, rsem, dev):
        pltpu.make_async_remote_copy(
            src_ref=dst, dst_ref=dst, send_sem=ssem, recv_sem=rsem,
            device_id=dev, device_id_type=MESH,
        ).wait_recv()

    barrier = pltpu.get_barrier_semaphore()
    peers = [zdev(d) for d in (4, -4, 3, -3, 2, -2, 1, -1)]
    peers += [pdev(wrap(yx + j, NP)) for j in range(1, NP)]
    peers.append(sibling)
    for dev in peers:
        pl.semaphore_signal(barrier, inc=1, device_id=dev, device_id_type=MESH)
    load = pltpu.make_async_copy(centers_ref, cbuf, csem)
    load.start()

    v = feat_ref[...].astype(jnp.float32)
    fq = lax.rsqrt(jnp.sum(v * v, axis=-1, keepdims=True) + norm_eps)
    xa[yx] = (v * fq).astype(jnp.bfloat16)

    load.wait()
    owner = z * (2 * NP) + cls
    for b in range(CLS // BLK):
        chosen[b * BLK:(b + 1) * BLK, :] = cbuf[sampled_ref[owner, b]]
    c = chosen[...]
    cq = lax.rsqrt(jnp.sum(c * c, axis=-1, keepdims=True) + norm_eps)
    wa[core, z] = (c * cq).astype(jnp.bfloat16)

    pl.semaphore_wait(barrier, len(peers))

    n = 0
    for d in DIRECT:
        send(wa.at[core, z], wa.at[core, z], z_send.at[n], z_recv.at[-d % NZ], zdev(d))
        n += 1
    for j in (2, 1, 3):
        send(xa.at[yx], xa.at[yx], a_send.at[j], a_recv.at[SIDE - j], pdev(chip(wrap(first + j, SIDE), second)))
    send(wa.at[core, z], wa.at[core, z], s_send.at[0], s_recv.at[0], sibling)

    for i in range(SIDE):
        slot = chip(wrap(first + i, SIDE), second)
        if i:
            arrived(xa.at[slot], a_send.at[i], a_recv.at[i], pdev(slot))
        for j in (2, 1, 3):
            send(xa.at[slot], xa.at[slot], b_send.at[j, i], b_recv.at[SIDE - j, i],
                 pdev(chip(first, wrap(second + j, SIDE))))

    def class_arrived(d):
        slot = wrap(z + d, NZ)
        arrived(wa.at[core, slot], z_send.at[0], z_recv.at[d % NZ], zdev(d))
        send(wa.at[core, slot], wa.at[core, slot], s_send.at[d % NZ], s_recv.at[d % NZ], sibling)
        return slot

    for d, nexts in ((-4, PASS_UP), (4, PASS_DOWN)):
        slot = class_arrived(d)
        for e in nexts:
            send(wa.at[core, slot], wa.at[core, slot], z_send.at[n], z_recv.at[(d - e) % NZ], zdev(e))
            n += 1
    sign = 1 - 2 * core
    slot = wrap(z - 4 * sign, NZ)
    send(wa.at[core, slot], wa.at[core, slot], z_send.at[n], z_recv.at[8], (wrap(z + 4 * sign, NZ), cls))
    for d in (1, -1, 2, -2, 3, -3, 5, -5, 6, -6, 7, -7, 8):
        class_arrived(d)

    for i in range(SIDE):
        for j in (1, 2, 3):
            slot = chip(wrap(first + i, SIDE), wrap(second + j, SIDE))
            arrived(xa.at[slot], b_send.at[j, i], b_recv.at[j, i], pdev(slot))
    for d in range(NZ):
        slot = wrap(z + d, NZ)
        arrived(wa.at[1 - core, slot], s_send.at[d], s_recv.at[d], sibling)

    xv = xa[...].reshape(TILE_ROWS, D)
    for k in range(4):
        w = wa[k // 2, (k % 2) * 8:(k % 2) * 8 + 8].reshape(256, D)
        et[k * 256:(k + 1) * 256, :] = lax.dot_general(
            w, xv, (((1,), (1,)), ((), ())), preferred_element_type=jnp.float32
        )
    lab = label_ref[...]
    step = lax.broadcasted_iota(jnp.int32, (BLK, TILE_ROWS), 0)

    def hits(b):
        zz = lax.div(lax.rem(b, 32), 2)
        o = zz * (2 * NP) + yx * 2 + lax.div(b, 32)
        base = (o * BLOCKS + sampled_ref[o, lax.rem(b, 2)]) * BLK
        return (lab - base) == step

    def score(b, carry):
        rows = pl.ds(pl.multiple_of(b * BLK, BLK), BLK)
        hit = hits(b)
        s = logit_scale * et[rows, :] - jnp.where(hit, logit_scale * cosine_margin, 0.0)
        e = jnp.exp(s)
        et[rows, :] = e
        return carry[0] + e, carry[1] + jnp.where(hit, s, 0.0)

    zero = jnp.zeros((BLK, TILE_ROWS), jnp.float32)
    esum, tsum = lax.fori_loop(0, 2 * 32, score, (zero, zero))
    tot[0] = jnp.sum(esum, axis=0, keepdims=True)
    tgt[0] = jnp.sum(tsum, axis=0, keepdims=True)
    for j in range(1, NP):
        dev = pdev(wrap(yx + j, NP))
        send(tot.at[0], tot.at[NP - j], t_send.at[j], t_recv.at[NP - j], dev)
    for j in range(1, NP):
        dev = pdev(wrap(yx + j, NP))
        send(tgt.at[0], tgt.at[NP - j], u_send.at[j], u_recv.at[NP - j], dev)
    for j in range(1, NP):
        arrived(tot.at[j], t_send.at[j], t_recv.at[j], pdev(wrap(yx + j, NP)))
    total = tot[0]
    for j in range(1, NP):
        total = total + tot[j]
    inverse = 1.0 / total

    def grad(b, carry):
        rows = pl.ds(pl.multiple_of(b * BLK, BLK), BLK)
        hit = hits(b)
        g = (et[rows, :] * inverse - jnp.where(hit, 1.0, 0.0)) * logit_scale
        gt[rows, :] = g.astype(jnp.bfloat16)
        return carry

    def center_part(half, k):
        rows = pl.ds(pl.multiple_of(half * 512 + k * 256, 256), 256)
        return jnp.dot(gt[rows, :], xv, preferred_element_type=jnp.float32)

    other = 1 - core
    lax.fori_loop(other * 32, other * 32 + 32, grad, 0)
    for k in range(2):
        sib_out[k * 8:k * 8 + 8] = center_part(other, k).astype(jnp.bfloat16).reshape(8, CLS, D)
        send(sib_out.at[pl.ds(k * 8, 8)], sib_in.at[pl.ds(k * 8, 8)], cs_send.at[k], cs_recv.at[k], sibling)
    lax.fori_loop(core * 32, core * 32 + 32, grad, 0)
    for k in range(2):
        p = center_part(core, k).reshape(8, CLS, D)
        arrived(sib_in.at[pl.ds(k * 8, 8)], cs_send.at[k], cs_recv.at[k], sibling)
        p = p + sib_in[k * 8:k * 8 + 8].astype(jnp.float32)
        part[k * 8:k * 8 + 8] = p
        part_b[k * 8:k * 8 + 8] = p.astype(jnp.bfloat16)

    n = 0

    def give(d, dst, rsem, dev):
        nonlocal n
        send(part_b.at[wrap(z + d, NZ)], dst, r_send.at[n], rsem, dev)
        n += 1

    for side, offs in ((0, FROM_LOW), (1, FROM_HIGH)):
        for i, o in enumerate(offs):
            give((-4, 4)[side] - o, relay_in.at[side, i], r_recv.at[side * 4 + i], zdev(-o))
    give(8, relay8.at[...], r_recv.at[8], (wrap(z - 4 * sign, NZ), cls))
    for i, d in enumerate((1, -1, 2, -2)):
        give(d, zfin.at[i], q_recv.at[i], zdev(d))

    wv = wa[...].reshape(TILE_CLS, D)
    for k in range(3):
        fval[k * 256:(k + 1) * 256, :] = lax.dot_general(
            gt[:, k * 256:(k + 1) * 256], wv, (((0,), (0,)), ((), ())), preferred_element_type=jnp.float32
        )
    fout[...] = fval[...].astype(jnp.bfloat16).reshape(NP, ROWS, D)
    for i in range(SIDE):
        for j in (2, 1, 3):
            slot = chip(wrap(first + i, SIDE), wrap(second + j, SIDE))
            send(fout.at[slot], fin1.at[SIDE - j, i], f_send.at[j, i], f_recv.at[SIDE - j, i],
                 pdev(chip(first, wrap(second + j, SIDE))))

    for side, offs in ((0, FROM_LOW), (1, FROM_HIGH)):
        for i, o in enumerate(offs):
            arrived(relay_in.at[side, i], r_send.at[0], r_recv.at[side * 4 + i], zdev(o))
    arrived(relay8.at[...], r_send.at[0], r_recv.at[8], (wrap(z + 4 * sign, NZ), cls))
    for side, d in ((0, -4), (1, 4)):
        acc = part[wrap(z + d, NZ)]
        for i in range(4):
            acc = acc + relay_in[side, i].astype(jnp.float32)
        acc = acc + jnp.where(core == side, relay8[...].astype(jnp.float32), 0.0)
        relay_out[side] = acc.astype(jnp.bfloat16)
        send(relay_out.at[side], zfin.at[4 + side], q_send.at[side], q_recv.at[4 + side], zdev(d))

    own_f = None
    for i in (1, 2, 3, 0):
        slot = chip(wrap(first + i, SIDE), second)
        acc = fval[pl.ds(pl.multiple_of(slot * ROWS, 16), ROWS), :]
        for j in (1, 2, 3):
            arrived(fin1.at[j, i], f_send.at[j, i], f_recv.at[j, i], pdev(chip(first, wrap(second + j, SIDE))))
            acc = acc + fin1[j, i].astype(jnp.float32)
        if i:
            fout2[i] = acc.astype(jnp.bfloat16)
            send(fout2.at[i], fin2.at[SIDE - i], h_send.at[i], h_recv.at[SIDE - i], pdev(slot))
        else:
            own_f = acc

    for j in range(1, NP):
        arrived(tgt.at[j], u_send.at[j], u_recv.at[j], pdev(wrap(yx + j, NP)))
    target = tgt[0]
    for j in range(1, NP):
        target = target + tgt[j]
    loss_ref[...] = jnp.log(total) - target

    def back(v, q, g):
        return g * q - v * (q * q * q * jnp.sum(v * g, axis=-1, keepdims=True))

    for i in (1, 2, 3):
        arrived(fin2.at[i], h_send.at[i], h_recv.at[i], pdev(chip(wrap(first + i, SIDE), second)))
        own_f = own_f + fin2[i].astype(jnp.float32)
    fgrad_ref[...] = back(v, fq, own_f)

    own_c = part[z]
    for i, d in enumerate((-1, 1, -2, 2, 4, -4)):
        arrived(zfin.at[i], q_send.at[0], q_recv.at[i], zdev(d))
        own_c = own_c + zfin[i].astype(jnp.float32)
    cgrad_ref[...] = back(c, cq, own_c)

    for copy in started:
        copy.wait_send()


def scratch():
    bf, f32, dma = jnp.bfloat16, jnp.float32, pltpu.SemaphoreType.DMA
    vm = pltpu.VMEM
    return [
        vm((BLOCKS, BLK, D), f32), vm((CLS, D), f32), vm((NP, ROWS, D), bf), vm((2, NZ, CLS, D), bf),
        vm((TILE_CLS, TILE_ROWS), f32), vm((TILE_CLS, TILE_ROWS), bf),
        vm((NP, 1, TILE_ROWS), f32), vm((NP, 1, TILE_ROWS), f32),
        vm((NZ, CLS, D), bf), vm((NZ, CLS, D), bf), vm((NZ, CLS, D), f32), vm((NZ, CLS, D), bf),
        vm((2, 4, CLS, D), bf), vm((CLS, D), bf), vm((2, CLS, D), bf), vm((6, CLS, D), bf),
        vm((TILE_ROWS, D), f32), vm((NP, ROWS, D), bf), vm((SIDE, SIDE, ROWS, D), bf),
        vm((SIDE, ROWS, D), bf), vm((SIDE, ROWS, D), bf),
        dma, dma((NZ,)), dma((NZ,)), dma((NZ,)), dma((NZ,)), dma((SIDE,)), dma((SIDE,)),
        dma((SIDE, SIDE)), dma((SIDE, SIDE)),
        dma((NP,)), dma((NP,)), dma((NP,)), dma((NP,)), dma((2,)), dma((2,)),
        dma((13,)), dma((9,)), dma((2,)), dma((6,)), dma((SIDE, SIDE)), dma((SIDE, SIDE)), dma((SIDE,)), dma((SIDE,)),
    ]


def local(features, centers, labels, sampled):
    dp_index = lax.axis_index("dp")
    cls_index = lax.axis_index("cls")
    plane_labels = labels.reshape(NZ, NP, 2, ROWS)
    own = lax.dynamic_slice(
        plane_labels, (dp_index, 0, lax.rem(cls_index, 2), 0), (1, NP, 1, ROWS)
    ).reshape(1, TILE_ROWS)
    vmem = pl.BlockSpec(memory_space=pltpu.VMEM)
    losses, feature_grad, center_grad = pl.pallas_call(
        kernel,
        out_shape=(
            jax.ShapeDtypeStruct((1, TILE_ROWS), jnp.float32),
            jax.ShapeDtypeStruct((ROWS, D), jnp.float32),
            jax.ShapeDtypeStruct((CLS, D), jnp.float32),
        ),
        in_specs=[vmem, pl.BlockSpec(memory_space=pl.ANY), vmem, pl.BlockSpec(memory_space=pltpu.SMEM)],
        out_specs=(vmem, vmem, vmem),
        scratch_shapes=scratch(),
        compiler_params=pltpu.CompilerParams(
            collective_id=0, has_side_effects=True, vmem_limit_bytes=48 * 1024 * 1024
        ),
        name="margin_step",
    )(features, centers.reshape(BLOCKS, BLK, D), own, sampled)
    losses = lax.dynamic_slice(losses.reshape(TILE_ROWS), (lax.div(cls_index, 2) * ROWS,), (ROWS,))
    return (losses, feature_grad, center_grad)


def solution(mesh):
    placed = (P(("dp", "cls"), None), P(("dp", "cls"), None), P(), P())
    return jax.shard_map(
        local,
        mesh=mesh,
        in_specs=placed,
        out_specs=(P(("dp", "cls")), P(("dp", "cls"), None), P(("dp", "cls"), None)),
        check_vma=False,
    )
```

time: 297 us -> 71.6 us (0.24)
  waiting for transfers between devices: 196 us -> 0 us
  Pallas kernels: 0 us -> 63.6 us
  blocking collectives: 61.4 us -> 0 us
  between operations: 13.9 us -> 0.69 us
  other arithmetic: 9.28 us -> 0 us
  matrix products: 8.94 us -> 0 us
    reduce_scatter x2 -> x0, waiting for transfers between devices: 172 us -> none  [the longest x1 113 us: local(): lax.psum_scatter(lax.dot_general(grad_logit, gathered_x, (((0,), (0,)), (...]
    pallas_call x0 -> x1, Pallas kernels: none -> 63.6 us  [local(): pl.pallas_call(kernel, out_shape=(jax.ShapeDtypeStruct((1, TILE_ROWS), jn...]
    all_gather x1 -> x0, blocking collectives: 36.3 us -> none  [local(): gathered_x = lax.all_gather(feature_unit, 'dp', axis=0, tiled=True)]
    psum x1 -> x0, blocking collectives: 25.1 us -> none  [local(): all_total, all_target = lax.psum((totals, targets), 'dp')]
    all_gather x1 -> x0, waiting for transfers between devices: 24.3 us -> none  [local(): gathered_w = lax.all_gather(center_unit, 'cls', axis=0, tiled=True)]
    dot_general x3 -> x0, matrix products: 8.94 us -> none  [the longest x1 3.78 us: local(): lax.dot_general(grad_logit, gathered_x, (((0,), (0,)), ((), ())), preferr...]
    unnamed x9 -> x7, local copies, waits for them, and re-layouts: 1.28 us -> 5.08 us
    add_any x2 -> x0, other arithmetic: 3.18 us -> none  [unit_rows(): values * values]
  transfers between devices with their start and end apart: 3 -> 0, of which waited for: 3 -> 0; matrix products, arithmetic and copies ran while one was open for 3% -> 0% of each run, Pallas kernels for 0% -> 0%
where the time goes in v1:
time: 71.6 us; the launch traced here: 71.3 us
  Pallas kernels  63.6 us (89%)
  local copies, waits for them, and re-layouts  7.1 us (10%)
    pallas_call x1, Pallas kernels, local(): pl.pallas_call(kernel, out_shape=(jax.ShapeDtypeStruct((1, TILE_ROWS), jn...  63.6 us
    unnamed x7, local copies, waits for them, and re-layouts  5.08 us

profile of v1, /device:TPU:1, one launch (start us, length us, event | category | flops | bytes accessed | tf_op | source)
XLA Modules:
  0.0 71.3 jit_solution(16664185385260876016)
XLA Ops:
  0.6 1.3 %reshape.18 = s32[16,16,2,48]{3,2,1,0:T(2,128)S(1)} reshape(s32[24576]{0:T(1024)} %param.6) | data formatting | bytes 196608 | tf_op jit(solution)/shard_map/reshape | solution.py:307
  2.0 0.1 reshape.19.label_ref
  2.1 0.8 %copy.8.sampled_ref = s32[512,2]{1,0:T(8,128)S(1)} copy(s32[512,2]{0,1:T(2,128)} %param.7) | data formatting | bytes 8192 | tf_op args[3]
  2.9 0.0 copy-start
  2.9 2.2 %copy-done = f32[2048,512]{1,0:T(8,128)S(1)} copy-done((f32[2048,512]{1,0:T(8,128)S(1)}, f32[2048,512]{1,0:T(8,128)}, u32[]{:S(2)}) %copy-start) | copy-done | bytes 4194328
  5.1 0.0 copy-start.1
  5.1 0.8 %copy-done.1 = bf16[48,512]{1,0:T(8,128)(2,1)S(1)} copy-done((bf16[48,512]{1,0:T(8,128)(2,1)S(1)}, bf16[48,512]{1,0:T(8,128)(2,1)}, u32[]{:S(2)}) %copy-start.1) | copy-done | bytes 49176
  5.9 63.6 %margin_step.1 = (f32[1,768]{1,0:T(1,128)S(1)}, f32[48,512]{1,0:T(8,128)S(1)}, f32[32,512]{1,0:T(8,128)S(1)}) custom-call(bf16[48,512]{1,0:T(8,128)(2,1)S(1)} %copy-done.1, f32[128,16,512]{2,1,0:T(8,128)S(1)} %bitcast.3, s32[1,768]{1,0:T(1,128)S(1)} %reshape.19.label_ref, s32[512,2]{1,0:T(8,128)S(1)} %copy.8.sampled_ref), custom_call_target="tpu_custom_call" | custom-call | tf_op jit(solution)/shard_map/margin_step/pallas_call | solution.py:312
  69.5 0.6 dynamic-slice_bitcast_fusion
  70.1 0.6 copy.11
  70.7 0.6 copy.12
  (1 shorter events, 0.0 us)
Async XLA Ops:
  2.9 2.2 %copy-start = (f32[2048,512]{1,0:T(8,128)S(1)}, f32[2048,512]{1,0:T(8,128)}, u32[]{:S(2)}) copy-start(f32[2048,512]{1,0:T(8,128)} %param.5) | copy-start | bytes 12582916
  5.1 0.8 %copy-start.1 = (bf16[48,512]{1,0:T(8,128)(2,1)S(1)}, bf16[48,512]{1,0:T(8,128)(2,1)}, u32[]{:S(2)}) copy-start(bf16[48,512]{1,0:T(8,128)(2,1)} %feat_ref.1) | copy-start | bytes 147460

commit v2 on v1

v2 whole, which is shorter than its diff:
```python
import functools

import jax
import jax.numpy as jnp
from jax import lax
from jax.experimental import pallas as pl
from jax.experimental.pallas import tpu as pltpu
from jax.sharding import PartitionSpec as P

MESH = pl.DeviceIdType.MESH
BLK = 16
D = 512
ROWS = 48
CLS = 32
NZ = 16
NP = 16
SIDE = 4
BLOCKS = 128
TILE_ROWS = NP * ROWS
TILE_CLS = 2 * NZ * CLS

logit_scale = 64.0
cosine_margin = 0.35
norm_eps = 1e-06

ORDER = (0, 1, -1, 3, -3, 2, -2, 4, -4, 6, -6, 5, -5, 7, -7, 8)
AT = {d % NZ: p for p, d in enumerate(ORDER)}


def wrap(value, size):
    return lax.rem(value + size, size)


def kernel(
    feat_hbm, centers_hbm, label_hbm, sampled_hbm,
    loss_ref, fgrad_ref, cgrad_ref,
    feat_ref, cbuf, label_ref, sampled_ref, base_ref, chosen, xa, wa, et, gt, tot, tgt,
    sib_out, sib_in, part, part_b, near6, near8, near3, out6, out3, zfin,
    fval, fout, fin1, fout2, fin2,
    in_sem, z_send, z_recv, s_send, s_recv, a_send, a_recv, b_send, b_recv,
    t_send, t_recv, u_send, u_recv, cs_send, cs_recv,
    r_send, r_recv, q_send, q_recv, f_send, f_recv, h_send, h_recv,
):
    z = lax.axis_index("dp")
    cls = lax.axis_index("cls")
    core = lax.rem(cls, 2)
    yx = lax.div(cls, 2)
    y = lax.div(yx, SIDE)
    x = lax.rem(yx, SIDE)
    first = jnp.where(core == 0, y, x)
    second = jnp.where(core == 0, x, y)

    def chip(p1, p2):
        return jnp.where(core == 0, p1 * SIDE + p2, p2 * SIDE + p1)

    def zdev(d):
        return (wrap(z + d, NZ), cls)

    def pdev(slot):
        return (z, slot * 2 + core)

    sibling = (z, yx * 2 + 1 - core)
    started = []

    def send(src, dst, ssem, rsem, dev):
        copy = pltpu.make_async_remote_copy(
            src_ref=src, dst_ref=dst, send_sem=ssem, recv_sem=rsem,
            device_id=dev, device_id_type=MESH,
        )
        copy.start()
        started.append(copy)

    def arrived(dst, ssem, rsem, dev):
        pltpu.make_async_remote_copy(
            src_ref=dst, dst_ref=dst, send_sem=ssem, recv_sem=rsem,
            device_id=dev, device_id_type=MESH,
        ).wait_recv()

    barrier = pltpu.get_barrier_semaphore()
    peers = [zdev(d) for d in (3, -3, 2, -2, 1, -1)]
    peers += [pdev(wrap(yx + j, NP)) for j in range(1, NP)]
    peers.append(sibling)
    loads = [
        pltpu.make_async_copy(src, dst, in_sem.at[i])
        for i, (src, dst) in enumerate(
            ((sampled_hbm, sampled_ref), (centers_hbm, cbuf), (feat_hbm, feat_ref), (label_hbm, label_ref))
        )
    ]
    for load in loads:
        load.start()
    for dev in peers:
        pl.semaphore_signal(barrier, inc=1, device_id=dev, device_id_type=MESH)

    loads[2].wait()
    v = feat_ref[...].astype(jnp.float32)
    fq = lax.rsqrt(jnp.sum(v * v, axis=-1, keepdims=True) + norm_eps)
    xa[yx] = (v * fq).astype(jnp.bfloat16)

    loads[0].wait()
    loads[1].wait()
    owner = z * (2 * NP) + cls
    for b in range(CLS // BLK):
        chosen[b * BLK:(b + 1) * BLK, :] = cbuf[sampled_ref[b, owner]]
    c = chosen[...]
    cq = lax.rsqrt(jnp.sum(c * c, axis=-1, keepdims=True) + norm_eps)
    wa[0, 0] = (c * cq).astype(jnp.bfloat16)

    pl.semaphore_wait(barrier, len(peers))

    sent = 0

    def pass_on(d, e, dev):
        nonlocal sent
        send(wa.at[0, AT[d % NZ]], wa.at[0, AT[(d - e) % NZ]], z_send.at[sent], z_recv.at[(d - e) % NZ], dev)
        sent += 1

    def to_sibling(d):
        p = AT[d % NZ]
        send(wa.at[0, p], wa.at[1, p], s_send.at[p], s_recv.at[p], sibling)

    def class_arrived(d):
        arrived(wa.at[0, AT[d % NZ]], z_send.at[0], z_recv.at[d % NZ], zdev(d))

    for e in (3, -3, 1, -1):
        pass_on(0, e, zdev(e))
    for j in (2, 1, 3):
        send(xa.at[yx], xa.at[yx], a_send.at[j], a_recv.at[SIDE - j], pdev(chip(wrap(first + j, SIDE), second)))
    to_sibling(0)

    loads[3].wait()
    flat = jnp.concatenate([label_ref[pl.ds(z * 12 + i, 1), :] for i in range(12)], axis=1)
    lab = jnp.concatenate(
        [
            jnp.where(core == 0, flat[:, k * 96:k * 96 + 48], flat[:, k * 96 + 48:k * 96 + 96])
            for k in range(NP)
        ],
        axis=1,
    )
    for half in range(2):
        line = yx * 2 + (core if half == 0 else 1 - core)
        for p, d in enumerate(ORDER):
            o = wrap(z + d, NZ) * (2 * NP) + line
            for b in range(2):
                base_ref[half * 32 + p * 2 + b] = (o * BLOCKS + sampled_ref[b, o]) * BLK

    for i in range(SIDE):
        slot = chip(wrap(first + i, SIDE), second)
        if i:
            arrived(xa.at[slot], a_send.at[i], a_recv.at[i], pdev(slot))
        for j in (2, 1, 3):
            send(xa.at[slot], xa.at[slot], b_send.at[j, i], b_recv.at[SIDE - j, i],
                 pdev(chip(first, wrap(second + j, SIDE))))

    for d in (-3, 3):
        class_arrived(d)
        for e in (-d, -d // 3, d // 3):
            pass_on(d, e, zdev(e))
    for d in (1, -1):
        class_arrived(d)
    for d in (-3, 3, 1, -1):
        to_sibling(d)
    for d in (-6, 6):
        class_arrived(d)
        for e in (-d // 6, d // 6):
            pass_on(d, e, zdev(e))
    up = 1 - 2 * core
    far = jnp.where(core == 0, AT[-6 % NZ], AT[6])
    send(wa.at[0, far], wa.at[0, AT[8]], z_send.at[sent], z_recv.at[8], (wrap(z + 2 * up, NZ), cls))
    for d in (-6, 6):
        to_sibling(d)
    for d in (2, -2, 4, -4):
        class_arrived(d)
        to_sibling(d)

    for i in range(SIDE):
        for j in (1, 2, 3):
            slot = chip(wrap(first + i, SIDE), wrap(second + j, SIDE))
            arrived(xa.at[slot], b_send.at[j, i], b_recv.at[j, i], pdev(slot))

    xv = xa[...].reshape(TILE_ROWS, D)
    step = lax.broadcasted_iota(jnp.int32, (BLK, TILE_ROWS), 0)

    def hits(b):
        return (lab - base_ref[b]) == step

    def score(b, carry):
        rows = pl.ds(pl.multiple_of(b * BLK, BLK), BLK)
        hit = hits(b)
        s = logit_scale * et[rows, :] - jnp.where(hit, logit_scale * cosine_margin, 0.0)
        e = jnp.exp(s)
        et[rows, :] = e
        return carry[0] + e, carry[1] + jnp.where(hit, s, 0.0)

    def scores(half, k, carry):
        w = wa[half, k * 8:k * 8 + 8].reshape(256, D)
        q = half * 2 + k
        et[q * 256:(q + 1) * 256, :] = lax.dot_general(
            w, xv, (((1,), (1,)), ((), ())), preferred_element_type=jnp.float32
        )
        return lax.fori_loop(q * 16, q * 16 + 16, score, carry)

    def from_sibling(k):
        for p in range(k * 8, k * 8 + 8):
            arrived(wa.at[1, p], s_send.at[p], s_recv.at[p], sibling)

    zero = jnp.zeros((BLK, TILE_ROWS), jnp.float32)
    sums = scores(0, 0, (zero, zero))
    for d in (5, -5, 7, -7, 8):
        class_arrived(d)
        to_sibling(d)
    from_sibling(0)
    sums = scores(1, 0, sums)
    sums = scores(0, 1, sums)
    from_sibling(1)
    esum, tsum = scores(1, 1, sums)
    tot[0] = jnp.sum(esum, axis=0, keepdims=True)
    tgt[0] = jnp.sum(tsum, axis=0, keepdims=True)
    for j in range(1, NP):
        dev = pdev(wrap(yx + j, NP))
        send(tot.at[0], tot.at[NP - j], t_send.at[j], t_recv.at[NP - j], dev)
    for j in range(1, NP):
        arrived(tot.at[j], t_send.at[j], t_recv.at[j], pdev(wrap(yx + j, NP)))
    total = tot[0]
    for j in range(1, NP):
        total = total + tot[j]
    inverse = 1.0 / total

    def grad(b, carry):
        rows = pl.ds(pl.multiple_of(b * BLK, BLK), BLK)
        hit = hits(b)
        g = (et[rows, :] * inverse - jnp.where(hit, 1.0, 0.0)) * logit_scale
        gt[rows, :] = g.astype(jnp.bfloat16)
        return carry

    def center_part(half, k):
        q = half * 2 + k
        return jnp.dot(gt[q * 256:(q + 1) * 256, :], xv, preferred_element_type=jnp.float32)

    lax.fori_loop(32, 64, grad, 0)
    for k in range(2):
        sib_out[k * 8:k * 8 + 8] = center_part(1, k).astype(jnp.bfloat16).reshape(8, CLS, D)
        send(sib_out.at[pl.ds(k * 8, 8)], sib_in.at[pl.ds(k * 8, 8)], cs_send.at[k], cs_recv.at[k], sibling)
    lax.fori_loop(0, 32, grad, 0)
    for k in range(2):
        p = center_part(0, k).reshape(8, CLS, D)
        arrived(sib_in.at[pl.ds(k * 8, 8)], cs_send.at[k], cs_recv.at[k], sibling)
        p = p + sib_in[k * 8:k * 8 + 8].astype(jnp.float32)
        part[k * 8:k * 8 + 8] = p
        part_b[k * 8:k * 8 + 8] = p.astype(jnp.bfloat16)

    given = 0

    def give(d, dst, rsem, dev):
        nonlocal given
        send(part_b.at[AT[d % NZ]], dst, r_send.at[given], rsem, dev)
        given += 1

    give(8, near8.at[...], r_recv.at[4], (wrap(z - 2 * up, NZ), cls))
    for side, s in ((0, 1), (1, -1)):
        give(-5 * s, near6.at[side, 0], r_recv.at[side * 2], zdev(s))
        give(-7 * s, near6.at[side, 1], r_recv.at[side * 2 + 1], zdev(-s))
    for side, s in ((0, 1), (1, -1)):
        give(-2 * s, near3.at[side, 0], r_recv.at[5 + side * 2], zdev(s))
        give(-4 * s, near3.at[side, 1], r_recv.at[6 + side * 2], zdev(-s))
    for side, s in ((0, 1), (1, -1)):
        give(s, zfin.at[side], q_recv.at[side], zdev(s))

    wv = wa[...].reshape(TILE_CLS, D)
    for k in range(3):
        fval[k * 256:(k + 1) * 256, :] = lax.dot_general(
            gt[:, k * 256:(k + 1) * 256], wv, (((0,), (0,)), ((), ())), preferred_element_type=jnp.float32
        )
    fout[...] = fval[...].astype(jnp.bfloat16).reshape(NP, ROWS, D)
    for i in range(SIDE):
        for j in (2, 1, 3):
            slot = chip(wrap(first + i, SIDE), wrap(second + j, SIDE))
            send(fout.at[slot], fin1.at[SIDE - j, i], f_send.at[j, i], f_recv.at[SIDE - j, i],
                 pdev(chip(first, wrap(second + j, SIDE))))

    for j in range(1, NP):
        send(tgt.at[0], tgt.at[NP - j], u_send.at[j], u_recv.at[NP - j], pdev(wrap(yx + j, NP)))

    arrived(near8.at[...], r_send.at[0], r_recv.at[4], (wrap(z + 2 * up, NZ), cls))
    for side, s in ((0, 1), (1, -1)):
        arrived(near6.at[side, 0], r_send.at[0], r_recv.at[side * 2], zdev(-s))
        arrived(near6.at[side, 1], r_send.at[0], r_recv.at[side * 2 + 1], zdev(s))
        acc = part[AT[-6 * s % NZ]] + near6[side, 0].astype(jnp.float32) + near6[side, 1].astype(jnp.float32)
        acc = acc + jnp.where(core == side, near8[...].astype(jnp.float32), 0.0)
        out6[side] = acc.astype(jnp.bfloat16)
        send(out6.at[side], near3.at[side, 2], q_send.at[side], r_recv.at[9 + side], zdev(-3 * s))

    own_f = None
    for i in (1, 2, 3, 0):
        slot = chip(wrap(first + i, SIDE), second)
        acc = fval[pl.ds(pl.multiple_of(slot * ROWS, 16), ROWS), :]
        for j in (1, 2, 3):
            arrived(fin1.at[j, i], f_send.at[j, i], f_recv.at[j, i], pdev(chip(first, wrap(second + j, SIDE))))
            acc = acc + fin1[j, i].astype(jnp.float32)
        if i:
            fout2[i] = acc.astype(jnp.bfloat16)
            send(fout2.at[i], fin2.at[SIDE - i], h_send.at[i], h_recv.at[SIDE - i], pdev(slot))
        else:
            own_f = acc

    for side, s in ((0, 1), (1, -1)):
        arrived(near3.at[side, 0], r_send.at[0], r_recv.at[5 + side * 2], zdev(-s))
        arrived(near3.at[side, 1], r_send.at[0], r_recv.at[6 + side * 2], zdev(s))
        arrived(near3.at[side, 2], q_send.at[0], r_recv.at[9 + side], zdev(3 * s))
        acc = part[AT[-3 * s % NZ]]
        for i in range(3):
            acc = acc + near3[side, i].astype(jnp.float32)
        out3[side] = acc.astype(jnp.bfloat16)
        send(out3.at[side], zfin.at[2 + side], q_send.at[2 + side], q_recv.at[2 + side], zdev(-3 * s))

    for j in range(1, NP):
        arrived(tgt.at[j], u_send.at[j], u_recv.at[j], pdev(wrap(yx + j, NP)))
    target = tgt[0]
    for j in range(1, NP):
        target = target + tgt[j]
    every = jnp.log(total) - target
    own_loss = every[:, :ROWS]
    for k in range(1, NP):
        own_loss = jnp.where(yx == k, every[:, k * ROWS:(k + 1) * ROWS], own_loss)
    loss_ref[...] = own_loss

    def back(v, q, g):
        return g * q - v * (q * q * q * jnp.sum(v * g, axis=-1, keepdims=True))

    for i in (1, 2, 3):
        arrived(fin2.at[i], h_send.at[i], h_recv.at[i], pdev(chip(wrap(first + i, SIDE), second)))
        own_f = own_f + fin2[i].astype(jnp.float32)
    fgrad_ref[...] = back(v, fq, own_f)

    own_c = part[0]
    for i, d in enumerate((-1, 1, 3, -3)):
        arrived(zfin.at[i], q_send.at[0], q_recv.at[i], zdev(d))
        own_c = own_c + zfin[i].astype(jnp.float32)
    cgrad_ref[...] = back(c, cq, own_c)

    for copy in started:
        copy.wait_send()


def hand_over(a_ref, b_ref, c_ref, a_out, b_out, c_out):
    a_out[...] = a_ref[...]
    b_out[...] = b_ref[...]
    c_out[...] = c_ref[...]


def scratch():
    bf, f32, dma = jnp.bfloat16, jnp.float32, pltpu.SemaphoreType.DMA
    vm = pltpu.VMEM
    return [
        vm((ROWS, D), bf), vm((BLOCKS, BLK, D), f32), vm((192, 128), jnp.int32),
        pltpu.SMEM((2, 2 * NZ * NP), jnp.int32), pltpu.SMEM((64,), jnp.int32),
        vm((CLS, D), f32), vm((NP, ROWS, D), bf), vm((2, NZ, CLS, D), bf),
        vm((TILE_CLS, TILE_ROWS), f32), vm((TILE_CLS, TILE_ROWS), bf),
        vm((NP, 1, TILE_ROWS), f32), vm((NP, 1, TILE_ROWS), f32),
        vm((NZ, CLS, D), bf), vm((NZ, CLS, D), bf), vm((NZ, CLS, D), f32), vm((NZ, CLS, D), bf),
        vm((2, 2, CLS, D), bf), vm((CLS, D), bf), vm((2, 3, CLS, D), bf),
        vm((2, CLS, D), bf), vm((2, CLS, D), bf), vm((4, CLS, D), bf),
        vm((TILE_ROWS, D), f32), vm((NP, ROWS, D), bf), vm((SIDE, SIDE, ROWS, D), bf),
        vm((SIDE, ROWS, D), bf), vm((SIDE, ROWS, D), bf),
        dma((4,)), dma((NZ,)), dma((NZ,)), dma((NZ,)), dma((NZ,)), dma((SIDE,)), dma((SIDE,)),
        dma((SIDE, SIDE)), dma((SIDE, SIDE)),
        dma((NP,)), dma((NP,)), dma((NP,)), dma((NP,)), dma((2,)), dma((2,)),
        dma((11,)), dma((11,)), dma((4,)), dma((4,)), dma((SIDE, SIDE)), dma((SIDE, SIDE)), dma((SIDE,)), dma((SIDE,)),
    ]


def local(features, centers, labels, sampled):
    hbm = pl.BlockSpec(memory_space=pltpu.HBM)
    vmem = pl.BlockSpec(memory_space=pltpu.VMEM)
    losses, feature_grad, center_grad = pl.pallas_call(
        kernel,
        out_shape=(
            jax.ShapeDtypeStruct((1, ROWS), jnp.float32),
            jax.ShapeDtypeStruct((ROWS, D), jnp.float32),
            jax.ShapeDtypeStruct((CLS, D), jnp.float32),
        ),
        in_specs=[hbm, hbm, hbm, hbm],
        out_specs=(vmem, vmem, vmem),
        scratch_shapes=scratch(),
        compiler_params=pltpu.CompilerParams(
            collective_id=0, has_side_effects=True, vmem_limit_bytes=62 * 1024 * 1024
        ),
        name="margin_step",
    )(features, centers.reshape(BLOCKS, BLK, D), labels.reshape(192, 128), sampled.T)
    losses, feature_grad, center_grad = pl.pallas_call(
        hand_over,
        out_shape=(
            jax.ShapeDtypeStruct((1, ROWS), jnp.float32),
            jax.ShapeDtypeStruct((ROWS, D), jnp.float32),
            jax.ShapeDtypeStruct((CLS, D), jnp.float32),
        ),
        in_specs=[vmem] * 3,
        out_specs=(vmem,) * 3,
        compiler_params=pltpu.CompilerParams(vmem_limit_bytes=62 * 1024 * 1024),
        name="hand_over",
    )(losses, feature_grad, center_grad)
    return (losses.reshape(ROWS), feature_grad, center_grad)


def solution(mesh):
    placed = (P(("dp", "cls"), None), P(("dp", "cls"), None), P(), P())
    return jax.shard_map(
        local,
        mesh=mesh,
        in_specs=placed,
        out_specs=(P(("dp", "cls")), P(("dp", "cls"), None), P(("dp", "cls"), None)),
        check_vma=False,
    )
```

time: 71.6 us -> 59.6 us (0.83)
  local copies, waits for them, and re-layouts: 7.1 us -> 0 us
  Pallas kernels: 63.6 us -> 58.6 us
    unnamed x7 -> x0, local copies, waits for them, and re-layouts: 5.08 us -> none
    pallas_call x1 -> x2, Pallas kernels: 63.6 us -> 58.6 us  [the longest x1 57 us: local(): pl.pallas_call(kernel, out_shape=(jax.ShapeDtypeStruct((1, ROWS), jnp.flo...]
    reshape x2 -> x0, local copies, waits for them, and re-layouts: 1.4 us -> none  [the longest x1 1.32 us: local(): plane_labels = labels.reshape(NZ, NP, 2, ROWS)]
where the time goes in v2:
time: 59.6 us; the launch traced here: 59.2 us
  Pallas kernels  58.6 us (98%)
  between operations  0.64 us (1%)
    pallas_call x1, Pallas kernels, local(): pl.pallas_call(kernel, out_shape=(jax.ShapeDtypeStruct((1, ROWS), jnp.flo...  57 us
    pallas_call x1, Pallas kernels, local(): pl.pallas_call(hand_over, out_shape=(jax.ShapeDtypeStruct((1, ROWS), jnp....  1.57 us

profile of v2, /device:TPU:1, one launch (start us, length us, event | category | flops | bytes accessed | tf_op | source)
XLA Modules:
  0.0 59.2 jit_solution(3483169900682098638)
XLA Ops:
  0.6 57.0 %margin_step.1 = (f32[1,48]{1,0:T(1,128)}, f32[48,512]{1,0:T(8,128)}, f32[32,512]{1,0:T(8,128)}) custom-call(bf16[48,512]{1,0:T(8,128)(2,1)} %feat_hbm.1, f32[128,16,512]{2,1,0:T(8,128)} %bitcast.4, s32[192,128]{1,0:T(8,128)} %bitcast.5, s32[2,512]{1,0:T(2,128)} %bitcast.6), custom_call_target="tpu_custom_call" | custom-call | tf_op jit(solution)/shard_map/margin_step/pallas_call | solution.py:374
  57.7 1.6 %hand_over.1 = (f32[1,48]{1,0:T(1,128)}, f32[48,512]{1,0:T(8,128)}, f32[32,512]{1,0:T(8,128)}) custom-call(f32[1,48]{1,0:T(1,128)} %get-tuple-element.9.a_ref, f32[48,512]{1,0:T(8,128)} %get-tuple-element.10.b_ref, f32[32,512]{1,0:T(8,128)} %get-tuple-element.11.c_ref), custom_call_target="tpu_custom_call" | custom-call | tf_op jit(solution)/shard_map/hand_over/pallas_call | solution.py:389

commit v3 on v2

--- a/solution.py
+++ b/solution.py
@@ -23,7 +23,7 @@
 cosine_margin = 0.35
 norm_eps = 1e-06
 
-ORDER = (0, 1, -1, 3, -3, 2, -2, 4, -4, 6, -6, 5, -5, 7, -7, 8)
+ORDER = (0, 1, -1, 3, -3, 2, -2, 6, -6, 4, -4, 5, -5, 7, -7, 8)
 AT = {d % NZ: p for p, d in enumerate(ORDER)}
 
 
@@ -34,9 +34,9 @@
 def kernel(
     feat_hbm, centers_hbm, label_hbm, sampled_hbm,
     loss_ref, fgrad_ref, cgrad_ref,
-    feat_ref, cbuf, label_ref, sampled_ref, base_ref, chosen, xa, wa, et, gt, tot, tgt,
+    feat_ref, cbuf, label_ref, sampled_ref, base_ref, chosen, xa, wa, et, gt, labcol, sn, en, hn, tot, tgt,
     sib_out, sib_in, part, part_b, near6, near8, near3, out6, out3, zfin,
-    fval, fout, fin1, fout2, fin2,
+    fval, hval, fout, fin1, fout2, fin2,
     in_sem, z_send, z_recv, s_send, s_recv, a_send, a_recv, b_send, b_recv,
     t_send, t_recv, u_send, u_recv, cs_send, cs_recv,
     r_send, r_recv, q_send, q_recv, f_send, f_recv, h_send, h_recv,
@@ -78,12 +78,15 @@
 
     barrier = pltpu.get_barrier_semaphore()
     peers = [zdev(d) for d in (3, -3, 2, -2, 1, -1)]
-    peers += [pdev(wrap(yx + j, NP)) for j in range(1, NP)]
+    peers += [pdev(chip(wrap(first + j, SIDE), second)) for j in (2, 1, 3)]
+    peers += [pdev(chip(first, wrap(second + j, SIDE))) for j in (2, 1, 3)]
     peers.append(sibling)
     loads = [
         pltpu.make_async_copy(src, dst, in_sem.at[i])
         for i, (src, dst) in enumerate(
-            ((sampled_hbm, sampled_ref), (centers_hbm, cbuf), (feat_hbm, feat_ref), (label_hbm, label_ref))
+            [(sampled_hbm, sampled_ref)]
+            + [(centers_hbm.at[pl.ds(k * 32, 32)], cbuf.at[pl.ds(k * 32, 32)]) for k in range(4)]
+            + [(feat_hbm, feat_ref), (label_hbm, label_ref)]
         )
     ]
     for load in loads:
@@ -91,13 +94,13 @@
     for dev in peers:
         pl.semaphore_signal(barrier, inc=1, device_id=dev, device_id_type=MESH)
 
-    loads[2].wait()
+    loads[5].wait()
     v = feat_ref[...].astype(jnp.float32)
     fq = lax.rsqrt(jnp.sum(v * v, axis=-1, keepdims=True) + norm_eps)
     xa[yx] = (v * fq).astype(jnp.bfloat16)
 
-    loads[0].wait()
-    loads[1].wait()
+    for load in loads[:5]:
+        load.wait()
     owner = z * (2 * NP) + cls
     for b in range(CLS // BLK):
         chosen[b * BLK:(b + 1) * BLK, :] = cbuf[sampled_ref[b, owner]]
@@ -127,7 +130,7 @@
         send(xa.at[yx], xa.at[yx], a_send.at[j], a_recv.at[SIDE - j], pdev(chip(wrap(first + j, SIDE), second)))
     to_sibling(0)
 
-    loads[3].wait()
+    loads[6].wait()
     flat = jnp.concatenate([label_ref[pl.ds(z * 12 + i, 1), :] for i in range(12)], axis=1)
     lab = jnp.concatenate(
         [
@@ -136,6 +139,7 @@
         ],
         axis=1,
     )
+    labcol[...] = jnp.transpose(jnp.broadcast_to(lab, (128, TILE_ROWS)))
     for half in range(2):
         line = yx * 2 + (core if half == 0 else 1 - core)
         for p, d in enumerate(ORDER):
@@ -157,19 +161,21 @@
             pass_on(d, e, zdev(e))
     for d in (1, -1):
         class_arrived(d)
-    for d in (-3, 3, 1, -1):
+    for d in (1, -1, 3, -3):
         to_sibling(d)
     for d in (-6, 6):
         class_arrived(d)
-        for e in (-d // 6, d // 6):
-            pass_on(d, e, zdev(e))
     up = 1 - 2 * core
     far = jnp.where(core == 0, AT[-6 % NZ], AT[6])
     send(wa.at[0, far], wa.at[0, AT[8]], z_send.at[sent], z_recv.at[8], (wrap(z + 2 * up, NZ), cls))
+    sent += 1
     for d in (-6, 6):
-        to_sibling(d)
+        for e in (-d // 6, d // 6):
+            pass_on(d, e, zdev(e))
     for d in (2, -2, 4, -4):
         class_arrived(d)
+        to_sibling(d)
+    for d in (-6, 6):
         to_sibling(d)
 
     for i in range(SIDE):
@@ -203,13 +209,38 @@
         for p in range(k * 8, k * 8 + 8):
             arrived(wa.at[1, p], s_send.at[p], s_recv.at[p], sibling)
 
+    lane = lax.broadcasted_iota(jnp.int32, (1, 128), 1)
+
+    def ids(at):
+        row = lax.rem(lane, BLK) + base_ref[at]
+        for j in range(1, 8):
+            row = jnp.where(lax.div(lane, BLK) == j, lax.rem(lane, BLK) + base_ref[at + j], row)
+        return row
+
+    def feature_part(k):
+        w = wa[:, k * 8:k * 8 + 8].reshape(512, D)
+        classes = [ids(half * 32 + k * 16 + j * 8) for half in range(2) for j in range(2)]
+        for i in range(3):
+            rows = slice(i * 256, (i + 1) * 256)
+            sn[...] = lax.dot_general(xv[rows, :], w, (((1,), (1,)), ((), ())), preferred_element_type=jnp.float32)
+            for g in range(4):
+                cols = slice(g * 128, (g + 1) * 128)
+                hit = labcol[rows, :] == classes[g]
+                e = jnp.exp(logit_scale * sn[:, cols] - jnp.where(hit, logit_scale * cosine_margin, 0.0))
+                en[:, cols] = e.astype(jnp.bfloat16)
+                hn[:, cols] = jnp.where(hit, 1.0, 0.0).astype(jnp.bfloat16)
+            for ref, lhs in ((fval, en), (hval, hn)):
+                more = jnp.dot(lhs[...], w, preferred_element_type=jnp.float32)
+                ref[rows, :] = more if k == 0 else ref[rows, :] + more
+
     zero = jnp.zeros((BLK, TILE_ROWS), jnp.float32)
     sums = scores(0, 0, (zero, zero))
+    from_sibling(0)
+    sums = scores(1, 0, sums)
+    feature_part(0)
     for d in (5, -5, 7, -7, 8):
         class_arrived(d)
         to_sibling(d)
-    from_sibling(0)
-    sums = scores(1, 0, sums)
     sums = scores(0, 1, sums)
     from_sibling(1)
     esum, tsum = scores(1, 1, sums)
@@ -218,6 +249,9 @@
     for j in range(1, NP):
         dev = pdev(wrap(yx + j, NP))
         send(tot.at[0], tot.at[NP - j], t_send.at[j], t_recv.at[NP - j], dev)
+
+    feature_part(1)
+
     for j in range(1, NP):
         arrived(tot.at[j], t_send.at[j], t_recv.at[j], pdev(wrap(yx + j, NP)))
     total = tot[0]
@@ -236,18 +270,6 @@
         q = half * 2 + k
         return jnp.dot(gt[q * 256:(q + 1) * 256, :], xv, preferred_element_type=jnp.float32)
 
-    lax.fori_loop(32, 64, grad, 0)
-    for k in range(2):
-        sib_out[k * 8:k * 8 + 8] = center_part(1, k).astype(jnp.bfloat16).reshape(8, CLS, D)
-        send(sib_out.at[pl.ds(k * 8, 8)], sib_in.at[pl.ds(k * 8, 8)], cs_send.at[k], cs_recv.at[k], sibling)
-    lax.fori_loop(0, 32, grad, 0)
-    for k in range(2):
-        p = center_part(0, k).reshape(8, CLS, D)
-        arrived(sib_in.at[pl.ds(k * 8, 8)], cs_send.at[k], cs_recv.at[k], sibling)
-        p = p + sib_in[k * 8:k * 8 + 8].astype(jnp.float32)
-        part[k * 8:k * 8 + 8] = p
-        part_b[k * 8:k * 8 + 8] = p.astype(jnp.bfloat16)
-
     given = 0
 
     def give(d, dst, rsem, dev):
@@ -255,28 +277,48 @@
         send(part_b.at[AT[d % NZ]], dst, r_send.at[given], rsem, dev)
         given += 1
 
+    def other_part(k):
+        lax.fori_loop(32 + k * 16, 48 + k * 16, grad, 0)
+        sib_out[k * 8:k * 8 + 8] = center_part(1, k).astype(jnp.bfloat16).reshape(8, CLS, D)
+        send(sib_out.at[pl.ds(k * 8, 8)], sib_in.at[pl.ds(k * 8, 8)], cs_send.at[k], cs_recv.at[k], sibling)
+
+    def own_part(k):
+        lax.fori_loop(k * 16, k * 16 + 16, grad, 0)
+        part[k * 8:k * 8 + 8] = center_part(0, k).reshape(8, CLS, D)
+
+    def add_up(k):
+        arrived(sib_in.at[pl.ds(k * 8, 8)], cs_send.at[k], cs_recv.at[k], sibling)
+        p = part[k * 8:k * 8 + 8] + sib_in[k * 8:k * 8 + 8].astype(jnp.float32)
+        part[k * 8:k * 8 + 8] = p
+        part_b[k * 8:k * 8 + 8] = p.astype(jnp.bfloat16)
+
+    other_part(1)
+    own_part(1)
+    other_part(0)
+    add_up(1)
     give(8, near8.at[...], r_recv.at[4], (wrap(z - 2 * up, NZ), cls))
     for side, s in ((0, 1), (1, -1)):
+        give(-7 * s, near6.at[side, 1], r_recv.at[side * 2 + 1], zdev(-s))
         give(-5 * s, near6.at[side, 0], r_recv.at[side * 2], zdev(s))
-        give(-7 * s, near6.at[side, 1], r_recv.at[side * 2 + 1], zdev(-s))
-    for side, s in ((0, 1), (1, -1)):
-        give(-2 * s, near3.at[side, 0], r_recv.at[5 + side * 2], zdev(s))
+    for side, s in ((0, 1), (1, -1)):
         give(-4 * s, near3.at[side, 1], r_recv.at[6 + side * 2], zdev(-s))
-    for side, s in ((0, 1), (1, -1)):
-        give(s, zfin.at[side], q_recv.at[side], zdev(s))
-
-    wv = wa[...].reshape(TILE_CLS, D)
-    for k in range(3):
-        fval[k * 256:(k + 1) * 256, :] = lax.dot_general(
-            gt[:, k * 256:(k + 1) * 256], wv, (((0,), (0,)), ((), ())), preferred_element_type=jnp.float32
-        )
-    fout[...] = fval[...].astype(jnp.bfloat16).reshape(NP, ROWS, D)
-    for i in range(SIDE):
+
+    column = jnp.transpose(jnp.broadcast_to(inverse, (8, TILE_ROWS)))[:, :1]
+    fsum = (fval[...] * column - hval[...]) * logit_scale
+    fval[...] = fsum
+    fout[...] = fsum.astype(jnp.bfloat16).reshape(NP, ROWS, D)
+    for i in (1, 2, 3, 0):
         for j in (2, 1, 3):
             slot = chip(wrap(first + i, SIDE), wrap(second + j, SIDE))
             send(fout.at[slot], fin1.at[SIDE - j, i], f_send.at[j, i], f_recv.at[SIDE - j, i],
                  pdev(chip(first, wrap(second + j, SIDE))))
 
+    own_part(0)
+    add_up(0)
+    for side, s in ((0, 1), (1, -1)):
+        give(-2 * s, near3.at[side, 0], r_recv.at[5 + side * 2], zdev(s))
+    for side, s in ((0, 1), (1, -1)):
+        give(s, zfin.at[side], q_recv.at[side], zdev(s))
     for j in range(1, NP):
         send(tgt.at[0], tgt.at[NP - j], u_send.at[j], u_recv.at[NP - j], pdev(wrap(yx + j, NP)))
 
@@ -287,7 +329,14 @@
         acc = part[AT[-6 * s % NZ]] + near6[side, 0].astype(jnp.float32) + near6[side, 1].astype(jnp.float32)
         acc = acc + jnp.where(core == side, near8[...].astype(jnp.float32), 0.0)
         out6[side] = acc.astype(jnp.bfloat16)
-        send(out6.at[side], near3.at[side, 2], q_send.at[side], r_recv.at[9 + side], zdev(-3 * s))
+        send(out6.at[side], zfin.at[4 + side], q_send.at[side], q_recv.at[4 + side], zdev(-6 * s))
+
+    for side, s in ((0, 1), (1, -1)):
+        arrived(near3.at[side, 0], r_send.at[0], r_recv.at[5 + side * 2], zdev(-s))
+        arrived(near3.at[side, 1], r_send.at[0], r_recv.at[6 + side * 2], zdev(s))
+        acc = part[AT[-3 * s % NZ]] + near3[side, 0].astype(jnp.float32) + near3[side, 1].astype(jnp.float32)
+        out3[side] = acc.astype(jnp.bfloat16)
+        send(out3.at[side], zfin.at[2 + side], q_send.at[2 + side], q_recv.at[2 + side], zdev(-3 * s))
 
     own_f = None
     for i in (1, 2, 3, 0):
@@ -302,16 +351,6 @@
         else:
             own_f = acc
 
-    for side, s in ((0, 1), (1, -1)):
-        arrived(near3.at[side, 0], r_send.at[0], r_recv.at[5 + side * 2], zdev(-s))
-        arrived(near3.at[side, 1], r_send.at[0], r_recv.at[6 + side * 2], zdev(s))
-        arrived(near3.at[side, 2], q_send.at[0], r_recv.at[9 + side], zdev(3 * s))
-        acc = part[AT[-3 * s % NZ]]
-        for i in range(3):
-            acc = acc + near3[side, i].astype(jnp.float32)
-        out3[side] = acc.astype(jnp.bfloat16)
-        send(out3.at[side], zfin.at[2 + side], q_send.at[2 + side], q_recv.at[2 + side], zdev(-3 * s))
-
     for j in range(1, NP):
         arrived(tgt.at[j], u_send.at[j], u_recv.at[j], pdev(wrap(yx + j, NP)))
     target = tgt[0]
@@ -332,7 +371,7 @@
     fgrad_ref[...] = back(v, fq, own_f)
 
     own_c = part[0]
-    for i, d in enumerate((-1, 1, 3, -3)):
+    for i, d in enumerate((-1, 1, 3, -3, 6, -6)):
         arrived(zfin.at[i], q_send.at[0], q_recv.at[i], zdev(d))
         own_c = own_c + zfin[i].astype(jnp.float32)
     cgrad_ref[...] = back(c, cq, own_c)
@@ -354,17 +393,18 @@
         vm((ROWS, D), bf), vm((BLOCKS, BLK, D), f32), vm((192, 128), jnp.int32),
         pltpu.SMEM((2, 2 * NZ * NP), jnp.int32), pltpu.SMEM((64,), jnp.int32),
         vm((CLS, D), f32), vm((NP, ROWS, D), bf), vm((2, NZ, CLS, D), bf),
-        vm((TILE_CLS, TILE_ROWS), f32), vm((TILE_CLS, TILE_ROWS), bf),
+        vm((TILE_CLS, TILE_ROWS), f32), vm((TILE_CLS, TILE_ROWS), bf), vm((TILE_ROWS, 128), jnp.int32),
+        vm((256, 512), f32), vm((256, 512), bf), vm((256, 512), bf),
         vm((NP, 1, TILE_ROWS), f32), vm((NP, 1, TILE_ROWS), f32),
         vm((NZ, CLS, D), bf), vm((NZ, CLS, D), bf), vm((NZ, CLS, D), f32), vm((NZ, CLS, D), bf),
-        vm((2, 2, CLS, D), bf), vm((CLS, D), bf), vm((2, 3, CLS, D), bf),
-        vm((2, CLS, D), bf), vm((2, CLS, D), bf), vm((4, CLS, D), bf),
-        vm((TILE_ROWS, D), f32), vm((NP, ROWS, D), bf), vm((SIDE, SIDE, ROWS, D), bf),
+        vm((2, 2, CLS, D), bf), vm((CLS, D), bf), vm((2, 2, CLS, D), bf),
+        vm((2, CLS, D), bf), vm((2, CLS, D), bf), vm((6, CLS, D), bf),
+        vm((TILE_ROWS, D), f32), vm((TILE_ROWS, D), f32), vm((NP, ROWS, D), bf), vm((SIDE, SIDE, ROWS, D), bf),
         vm((SIDE, ROWS, D), bf), vm((SIDE, ROWS, D), bf),
-        dma((4,)), dma((NZ,)), dma((NZ,)), dma((NZ,)), dma((NZ,)), dma((SIDE,)), dma((SIDE,)),
+        dma((7,)), dma((NZ,)), dma((NZ,)), dma((NZ,)), dma((NZ,)), dma((SIDE,)), dma((SIDE,)),
         dma((SIDE, SIDE)), dma((SIDE, SIDE)),
         dma((NP,)), dma((NP,)), dma((NP,)), dma((NP,)), dma((2,)), dma((2,)),
-        dma((11,)), dma((11,)), dma((4,)), dma((4,)), dma((SIDE, SIDE)), dma((SIDE, SIDE)), dma((SIDE,)), dma((SIDE,)),
+        dma((11,)), dma((9,)), dma((4,)), dma((6,)), dma((SIDE, SIDE)), dma((SIDE, SIDE)), dma((SIDE,)), dma((SIDE,)),
     ]
 
 

time: 59.6 us -> 57.2 us (0.960); the launches traced: 59.2 us -> 56.1 us
  Pallas kernels: 58.6 us -> 55.5 us
    pallas_call x1, Pallas kernels: 57 us -> 53.9 us  [local(): pl.pallas_call(kernel, out_shape=(jax.ShapeDtypeStruct((1, ROWS), jnp.flo...]
where the time goes in v3:
time: 57.2 us; the launch traced here: 56.1 us
  Pallas kernels  55.5 us (97%)
  between operations  0.64 us (1%)
    pallas_call x1, Pallas kernels, local(): pl.pallas_call(kernel, out_shape=(jax.ShapeDtypeStruct((1, ROWS), jnp.flo...  53.9 us
    pallas_call x1, Pallas kernels, local(): pl.pallas_call(hand_over, out_shape=(jax.ShapeDtypeStruct((1, ROWS), jnp....  1.57 us

profile of v3, /device:TPU:1, one launch (start us, length us, event | category | flops | bytes accessed | tf_op | source)
XLA Modules:
  0.0 56.1 jit_solution(352101277431918470)
XLA Ops:
  0.6 53.9 %margin_step.1 = (f32[1,48]{1,0:T(1,128)}, f32[48,512]{1,0:T(8,128)}, f32[32,512]{1,0:T(8,128)}) custom-call(bf16[48,512]{1,0:T(8,128)(2,1)} %feat_hbm.1, f32[128,16,512]{2,1,0:T(8,128)} %bitcast.4, s32[192,128]{1,0:T(8,128)} %bitcast.5, s32[2,512]{1,0:T(2,128)} %bitcast.6), custom_call_target="tpu_custom_call" | custom-call | tf_op jit(solution)/shard_map/margin_step/pallas_call | solution.py:414
  54.6 1.6 %hand_over.1 = (f32[1,48]{1,0:T(1,128)}, f32[48,512]{1,0:T(8,128)}, f32[32,512]{1,0:T(8,128)}) custom-call(f32[1,48]{1,0:T(1,128)} %get-tuple-element.9.a_ref, f32[48,512]{1,0:T(8,128)} %get-tuple-element.10.b_ref, f32[32,512]{1,0:T(8,128)} %get-tuple-element.11.c_ref), custom_call_target="tpu_custom_call" | custom-call | tf_op jit(solution)/shard_map/hand_over/pallas_call | solution.py:429

commit v4 on v3

--- a/solution.py
+++ b/solution.py
@@ -322,6 +322,8 @@
     for j in range(1, NP):
         send(tgt.at[0], tgt.at[NP - j], u_send.at[j], u_recv.at[NP - j], pdev(wrap(yx + j, NP)))
 
+    before = len(started)
+
     arrived(near8.at[...], r_send.at[0], r_recv.at[4], (wrap(z + 2 * up, NZ), cls))
     for side, s in ((0, 1), (1, -1)):
         arrived(near6.at[side, 0], r_send.at[0], r_recv.at[side * 2], zdev(-s))
@@ -337,6 +339,9 @@
         acc = part[AT[-3 * s % NZ]] + near3[side, 0].astype(jnp.float32) + near3[side, 1].astype(jnp.float32)
         out3[side] = acc.astype(jnp.bfloat16)
         send(out3.at[side], zfin.at[2 + side], q_send.at[2 + side], q_recv.at[2 + side], zdev(-3 * s))
+
+    last = started[before:]
+    del started[before:]
 
     own_f = None
     for i in (1, 2, 3, 0):
@@ -370,13 +375,15 @@
         own_f = own_f + fin2[i].astype(jnp.float32)
     fgrad_ref[...] = back(v, fq, own_f)
 
+    for copy in started:
+        copy.wait_send()
     own_c = part[0]
     for i, d in enumerate((-1, 1, 3, -3, 6, -6)):
         arrived(zfin.at[i], q_send.at[0], q_recv.at[i], zdev(d))
         own_c = own_c + zfin[i].astype(jnp.float32)
     cgrad_ref[...] = back(c, cq, own_c)
 
-    for copy in started:
+    for copy in last:
         copy.wait_send()
 
 

time: 57.2 us -> 57 us (level)
  no operation moved by 1% of the time
where the time goes in v4:
time: 57 us; the launch traced here: 56 us
  Pallas kernels  55.3 us (97%)
  between operations  0.64 us (1%)
    pallas_call x1, Pallas kernels, local(): pl.pallas_call(kernel, out_shape=(jax.ShapeDtypeStruct((1, ROWS), jnp.flo...  53.8 us
    pallas_call x1, Pallas kernels, local(): pl.pallas_call(hand_over, out_shape=(jax.ShapeDtypeStruct((1, ROWS), jnp....  1.57 us

profile of v4, /device:TPU:1, one launch (start us, length us, event | category | flops | bytes accessed | tf_op | source)
XLA Modules:
  0.0 56.0 jit_solution(6717529954184817645)
XLA Ops:
  0.6 53.8 %margin_step.1 = (f32[1,48]{1,0:T(1,128)}, f32[48,512]{1,0:T(8,128)}, f32[32,512]{1,0:T(8,128)}) custom-call(bf16[48,512]{1,0:T(8,128)(2,1)} %feat_hbm.1, f32[128,16,512]{2,1,0:T(8,128)} %bitcast.4, s32[192,128]{1,0:T(8,128)} %bitcast.5, s32[2,512]{1,0:T(2,128)} %bitcast.6), custom_call_target="tpu_custom_call" | custom-call | tf_op jit(solution)/shard_map/margin_step/pallas_call | solution.py:421
  54.4 1.6 %hand_over.1 = (f32[1,48]{1,0:T(1,128)}, f32[48,512]{1,0:T(8,128)}, f32[32,512]{1,0:T(8,128)}) custom-call(f32[1,48]{1,0:T(1,128)} %get-tuple-element.9.a_ref, f32[48,512]{1,0:T(8,128)} %get-tuple-element.10.b_ref, f32[32,512]{1,0:T(8,128)} %get-tuple-element.11.c_ref), custom_call_target="tpu_custom_call" | custom-call | tf_op jit(solution)/shard_map/hand_over/pallas_call | solution.py:436
